TPU v7x, 32 devices: a whole 2x2x4 slice. The times are simulated.
32 devices in a mesh: tx: 16 (over z, y, x), rx: 2 (over core).
Axes of the slice: x: 2, y: 2, z: 4, core: 2. Of those that a mesh axis runs over, the one named last changes fastest.
Arguments:
- captures: bfloat16 [128, 128, 256], P('tx', 'rx'), may hold values from -6 to 6
- elem_grid: int32 [2, 128], replicated, may hold values from 0 to 31, as said below
- excitation: int32 [64], replicated, may hold values from -1 to 1, as said below
- voxels: int32 [3, 512], replicated, may hold values from 0 to 63
Outputs:
- focused_image: float32 [2, 512], P(None, ('tx', 'rx'))
Inputs may be any that keep to these rules, and one draw needn't show every extreme that they name: `elem_grid`: every position of the probe's grid of 4 rows and 32 columns holds exactly one element. `excitation`: each tap is -1 or +1.
All inputs are finite; a program needn't handle non-finite values.
Results may differ from a plain program's by a relative error of at most 0.008.
Values may be sent and summed in bfloat16 or wider, within the bound.
A program may use at most 64 MiB of HBM per device.

v0:
```python
import math

import jax
import jax.numpy as jnp
from jax import lax
from jax.sharding import PartitionSpec as P

BINS = 8


samples_per_mm = 8.4746
pitch_mm = 0.5
power_floor = 0.1


def filter_table(excitation, gate_len, bin_count):
    tap_count = excitation.shape[0]
    first_bin = gate_len // 12
    lag_index = (
        jnp.arange(gate_len, dtype=jnp.int32)[:, None]
        - jnp.arange(tap_count, dtype=jnp.int32)[None, :]
    )
    frequency = first_bin + jnp.arange(bin_count, dtype=jnp.int32)
    phase_turns = jnp.mod(lag_index[:, :, None] * frequency[None, None, :], gate_len)
    phases = 2.0 * math.pi / gate_len * phase_turns.astype(jnp.float32)
    weight = jnp.where(lag_index >= 0, excitation[None, :], 0).astype(jnp.float32)[:, :, None]
    norm_scale = 1.0 / math.sqrt(tap_count * gate_len)
    real_part = jnp.sum(weight * jnp.cos(phases), axis=1) * norm_scale
    imag_part = -jnp.sum(weight * jnp.sin(phases), axis=1) * norm_scale
    return jnp.concatenate([real_part, imag_part], axis=1).astype(jnp.bfloat16)


def element_points(grid_cells, grid_rows):
    elem_x = (grid_cells[0].astype(jnp.float32) - 0.5 * (grid_rows - 1)) * pitch_mm
    elem_y = (grid_cells[1].astype(jnp.float32) - 15.5) * pitch_mm
    return (elem_x, elem_y)


def voxel_points(block_cells):
    cells_float = block_cells.astype(jnp.float32)
    return (
        (cells_float[0] - 31.5) * 0.5,
        (cells_float[1] - 31.5) * 0.5,
        10.0 + cells_float[2] * 0.5,
    )


def steer_angle(elem_x, elem_y, vox_x, vox_y, vox_z, frequency, gate_len):
    distance = jnp.sqrt(
        (elem_x[:, None] - vox_x[None, :]) ** 2
        + (elem_y[:, None] - vox_y[None, :]) ** 2
        + vox_z[None, :] ** 2
    )
    delay = distance * (samples_per_mm / gate_len)
    return 2.0 * math.pi * frequency.astype(jnp.float32)[:, None, None] * delay[None]


def local(captures, elem_grid, excitation, voxels):
    tx_count = lax.axis_size("tx")
    rx_count = lax.axis_size("rx")
    tx_rows, rx_cols, gate_len = captures.shape
    subrun = rx_cols // tx_count
    channels = 2 * BINS
    elements = tx_rows * tx_count
    matched = filter_table(excitation, gate_len, BINS)
    pieces = captures.reshape(rx_count, subrun, tx_count, subrun, gate_len)
    local_spec = jnp.einsum(
        "bhaxs,sc->cbhax", pieces, matched, preferred_element_type=jnp.float32
    ).astype(jnp.bfloat16)
    arrived = lax.all_to_all(
        lax.all_to_all(pieces, "tx", split_axis=2, concat_axis=2, tiled=True),
        "rx",
        split_axis=0,
        concat_axis=0,
        tiled=True,
    )
    mirror = jnp.einsum(
        "bhgxs,sc->cbxgh", arrived, matched, preferred_element_type=jnp.float32
    ).astype(jnp.bfloat16)
    averaged = ((local_spec.astype(jnp.float32) + mirror.astype(jnp.float32)) * 0.5).reshape(
        channels, tx_rows, rx_cols
    )
    power = jnp.mean(averaged * averaged, axis=0, keepdims=True)
    whitened = (
        (averaged / jnp.sqrt(jnp.maximum(power, power_floor)))
        .astype(jnp.bfloat16)
        .reshape(2, BINS, tx_rows, rx_cols)
    )
    left_side = jnp.concatenate([whitened[0], whitened[1]], axis=2)
    tx_cells = lax.dynamic_slice_in_dim(elem_grid, lax.axis_index("tx") * tx_rows, tx_rows, axis=1)
    rx_cells = lax.dynamic_index_in_dim(
        elem_grid.reshape(2, tx_count, rx_count, subrun),
        lax.axis_index("rx"),
        axis=2,
        keepdims=False,
    ).reshape(2, rx_cols)
    send_x, send_y = element_points(tx_cells, elements // 32)
    recv_x, recv_y = element_points(rx_cells, elements // 32)
    frequency = gate_len // 12 + jnp.arange(BINS, dtype=jnp.int32)
    voxel_count = voxels.shape[1]
    block_width = min(512, voxel_count)
    voxel_blocks = voxels.reshape(3, voxel_count // block_width, block_width).transpose(1, 0, 2)

    def image_block(block_cells):
        vox_x, vox_y, vox_z = voxel_points(block_cells)
        recv_phase = steer_angle(recv_x, recv_y, vox_x, vox_y, vox_z, frequency, gate_len)
        rx_cosine = jnp.cos(recv_phase).astype(jnp.bfloat16)
        rx_sine = jnp.sin(recv_phase).astype(jnp.bfloat16)
        steer_rx = jnp.concatenate(
            [
                jnp.concatenate([rx_cosine, rx_sine], axis=2),
                jnp.concatenate([-rx_sine, rx_cosine], axis=2),
            ],
            axis=1,
        )
        products = jnp.einsum(
            "ftl,flv->ftv", left_side, steer_rx, preferred_element_type=jnp.float32
        )
        prod_real = products[:, :, :block_width]
        prod_imag = products[:, :, block_width:]
        send_phase = steer_angle(send_x, send_y, vox_x, vox_y, vox_z, frequency, gate_len)
        tx_cosine = jnp.cos(send_phase)
        tx_sine = jnp.sin(send_phase)
        image_real = jnp.sum(prod_real * tx_cosine - prod_imag * tx_sine, axis=(0, 1))
        image_imag = jnp.sum(prod_real * tx_sine + prod_imag * tx_cosine, axis=(0, 1))
        return jnp.stack([image_real, image_imag])

    blocks = lax.map(image_block, voxel_blocks)
    partial_value = blocks.transpose(1, 0, 2).reshape(2, voxel_count) * (
        1.0 / (elements * math.sqrt(BINS))
    )
    image_part = lax.psum_scatter(partial_value, ("tx", "rx"), scatter_dimension=1, tiled=True)
    return image_part


def solution(mesh):
    placed = (P("tx", "rx", None), P(), P(), P())
    return jax.shard_map(
        local, mesh=mesh, in_specs=placed, out_specs=P(None, ("tx", "rx")), check_vma=False
    )
```

profile of v0, /device:TPU:0, one launch (start us, length us, event | category | flops | bytes accessed | tf_op | source)
XLA Modules:
  0.0 178.9 jit_solution(17944031101979596618)
XLA Ops:
  6.5 1.0 reshape.295
  7.6 0.0 copy-start.2
  7.6 0.0 copy-start.1
  7.6 0.0 copy-start
  7.6 0.8 copy.20
  8.4 8.3 %all-to-all-start = ((bf16[2,4,16,4,256]{4,3,1,0,2:T(4,128)(2,1)}), bf16[2,4,16,4,256]{4,3,1,0,2:T(4,128)(2,1)S(1)}, u32[]{:S(2)}, u32[]{:S(2)}) async-start(bf16[2,4,16,4,256]{4,3,1,0,2:T(4,128)(2,1)} %copy.20), calls=%async_computation | async-start | bytes 524288 | tf_op jit(solution)/shard_map/all_to_all | solution.py:71
  16.7 0.0 reduce-scatter.4.cloned.1.call-start
  16.8 0.1 select_convert_fusion
  16.9 0.1 reshape.297
  17.0 0.1 fusion.38
  17.1 0.1 mul.223
  17.2 0.1 mul.227
  17.3 0.1 constant_dynamic-slice_fusion
  17.4 2.4 %multiply_reduce_fusion.1 = (f32[256,8]{0,1:T(8,128)S(1)}, f32[256,8]{0,1:T(8,128)S(1)}) fusion(s32[8]{0:T(128)S(1)} %iota_add_fusion, s32[256,64]{0,1:T(8,128)S(1)} %iota_subtract_fusion, f32[256,64]{0,1:T(8,128)S(1)} %select_convert_fusion), kind=kLoop, calls=%fused_computation.28 | loop fusion | flops 2355200 | bytes 147488 | tf_op jit(solution)/shard_map/reduce_sum | solution.py:28
  19.9 0.1 sqrt_multiply_fusion
  20.0 3.6 %fusion.31 = bf16[8,64,512]{2,1,0:T(8,128)(2,1)S(1)} fusion(f32[64,512]{1,0:T(8,128)S(1)} %sqrt_multiply_fusion, f32[8]{0:T(128)S(1)} %convert_multiply_fusion), kind=kLoop, calls=%fused_computation.51 | loop fusion | flops 1310720 | bytes 655392 | tf_op jit(solution)/shard_map/while/body/eval_jaxpr/neg | solution.py:112
  23.7 0.1 sqrt_multiply_fusion.1
  23.8 0.4 fusion.12
  24.2 4.1 %fusion.14 = (bf16[8,64,512]{2,1,0:T(8,128)(2,1)S(1)}, bf16[8,64,512]{2,1,0:T(8,128)(2,1)S(1)}) fusion(f32[64,512]{1,0:T(8,128)S(1)} %sqrt_multiply_fusion, f32[8]{0:T(128)S(1)} %convert_multiply_fusion), kind=kLoop, calls=%fused_computation.18 | loop fusion | flops 786432 | bytes 1179680 | tf_op jit(solution)/shard_map/while/body/eval_jaxpr/convert_element_type | solution.py:108
  28.2 0.1 copy.21
  28.4 3.9 %all_to_all.10 = bf16[2,4,16,4,256]{4,2,3,1,0:T(8,128)(2,1)S(1)} all-to-all(bf16[2,4,16,4,256]{4,2,3,1,0:T(8,128)(2,1)S(1)} %copy.21), channel_id=1, replica_groups=mesh['tx'=16,'rx'=2] {'rx'}, dimensions={0} | all-to-all | bytes 524288 | tf_op jit(solution)/shard_map/all_to_all | solution.py:70
  32.3 0.4 multiply_reduce_fusion.2
  32.8 0.1 copy.23
  32.9 0.1 copy.25
  33.1 0.1 copy.24
  33.2 0.1 sqrt.28
  33.3 0.6 fusion
  34.0 0.6 fusion.25
  34.6 0.9 copy.30
  35.4 0.0 reduce-scatter.4.cloned.1.call-update
  35.5 135.3 %reduce-scatter.4.cloned.1.call-done = f32[16,2]{1,0:T(8,128)} async-done(((f32[512,2]{1,0:T(8,128)}), f32[16,2]{1,0:T(8,128)}) %reduce-scatter.4.cloned.1.call-update) | async-done | bytes 144
  170.7 1.3 copy.31
  (15 shorter events, 0.1 us)
Async XLA Ops:
  7.6 9.3 %copy-start.2 = (s32[64]{0:T(128)S(1)}, s32[64]{0:T(128)}, u32[]{:S(2)}) copy-start(s32[64]{0:T(128)} %param.6) | copy-start | bytes 772
  7.6 9.3 %copy-start.1 = (s32[2,128]{1,0:T(2,128)S(1)}, s32[2,128]{1,0:T(2,128)}, u32[]{:S(2)}) copy-start(s32[2,128]{1,0:T(2,128)} %param.5) | copy-start | bytes 3076
  7.6 9.7 %copy-start = (s32[3,512]{1,0:T(4,128)S(1)}, s32[3,512]{1,0:T(4,128)}, u32[]{:S(2)}) copy-start(s32[3,512]{1,0:T(4,128)} %param.7) | copy-start | bytes 18436
  8.4 19.8 %all-to-all-start = ((bf16[2,4,16,4,256]{4,3,1,0,2:T(4,128)(2,1)}), bf16[2,4,16,4,256]{4,3,1,0,2:T(4,128)(2,1)S(1)}, u32[]{:S(2)}, u32[]{:S(2)}) async-start(bf16[2,4,16,4,256]{4,3,1,0,2:T(4,128)(2,1)} %copy.20), calls=%async_computation | async-start | bytes 524288 | tf_op jit(solution)/shard_map/all_to_all | solution.py:71
  16.7 154.0 %reduce-scatter.4.cloned.1.call-start = ((), (), s32[]{:S(2)}) async-start(), calls=%async_computation.3 | async-start | bytes 270336
Sparse Core Ops, SparseCore 0:
  35.6 135.1 reduce-scatter.3
where the time goes:
time: 179 us
  waiting for transfers between devices  135 us (75%)
  between operations  13.6 us (8%)
  other arithmetic  11.2 us (6%)
  starting transfers between devices  8.35 us (5%)
  local copies, waits for them, and re-layouts  5.04 us (3%)
  blocking collectives  3.94 us (2%)
    unnamed x2, waiting for transfers between devices  135 us
    all_to_all x1, starting transfers between devices, local(): lax.all_to_all(pieces, 'tx', split_axis=2, concat_axis=2, tiled=True)  8.31 us
    convert_element_type x1, other arithmetic, image_block(): rx_sine = jnp.sin(recv_phase).astype(jnp.bfloat16)  4.05 us
    all_to_all x1, blocking collectives, local(): lax.all_to_all(lax.all_to_all(pieces, 'tx', split_axis=2, concat_axis=2,...  3.94 us
    neg x1, other arithmetic, image_block(): -rx_sine  3.63 us
  transfers between devices with their start and end apart: 2, of which 1 were waited for; matrix products, arithmetic and copies ran while one was open for 6% of the time, Pallas kernels for 0%

commit v1 on v0

--- a/solution.py
+++ b/solution.py
@@ -1,11 +1,16 @@
+import functools
 import math
 
 import jax
 import jax.numpy as jnp
+import numpy as np
 from jax import lax
+from jax.experimental import pallas as pl
+from jax.experimental.pallas import tpu as pltpu
 from jax.sharding import PartitionSpec as P
 
 BINS = 8
+LANES = 128
 
 
 samples_per_mm = 8.4746
@@ -55,7 +60,7 @@
     return 2.0 * math.pi * frequency.astype(jnp.float32)[:, None, None] * delay[None]
 
 
-def local(captures, elem_grid, excitation, voxels):
+def general(captures, elem_grid, excitation, voxels):
     tx_count = lax.axis_size("tx")
     rx_count = lax.axis_size("rx")
     tx_rows, rx_cols, gate_len = captures.shape
@@ -133,6 +138,336 @@
     return image_part
 
 
+def cosine_fit():
+    grid = np.cos(np.pi * (np.arange(400) + 0.5) / 400) * 0.125 + 0.125
+    fit = np.polynomial.chebyshev.Chebyshev.fit(
+        grid, np.cos(2.0 * np.pi * np.sqrt(grid)), 8, domain=[0.0, 0.25]
+    )
+    return [float(c) for c in fit.convert(kind=np.polynomial.Polynomial).coef]
+
+
+COSINE = cosine_fit()
+
+
+def cos_turns(turns):
+    rest = turns - jnp.floor(turns + 0.5)
+    square = rest * rest
+    total = jnp.full_like(square, COSINE[-1])
+    for factor in COSINE[-2::-1]:
+        total = total * square + factor
+    return total
+
+
+def iota(shape, axis):
+    return lax.broadcasted_iota(jnp.int32, shape, axis)
+
+
+def one_hot(mask):
+    return jnp.where(mask, 1.0, 0.0).astype(jnp.bfloat16)
+
+
+def matmul(left, right):
+    return jnp.dot(left, right, preferred_element_type=jnp.float32)
+
+
+def filter_lanes(excitation, gate_len):
+    taps = excitation.shape[1]
+    first_bin = gate_len // 12
+
+    def turns(rows):
+        lane = iota((rows, LANES), 1)
+        step = iota((rows, LANES), 0) * (first_bin + (lane & (BINS - 1)))
+        return (step & (gate_len - 1)).astype(jnp.float32) * (1.0 / gate_len), lane
+
+    tap_turns, _ = turns(taps)
+    tables = jnp.concatenate([cos_turns(tap_turns), cos_turns(tap_turns - 0.25)], axis=1)
+    high = tables.astype(jnp.bfloat16)
+    rest = tables - high.astype(jnp.float32)
+    middle = rest.astype(jnp.bfloat16)
+    low = (rest - middle.astype(jnp.float32)).astype(jnp.bfloat16)
+    reached = iota((gate_len, taps), 1) <= iota((gate_len, taps), 0)
+    weight = jnp.where(reached, excitation.astype(jnp.float32), 0.0).astype(jnp.bfloat16)
+    sums = matmul(weight, high) + (matmul(weight, middle) + matmul(weight, low))
+    gate_turns, lane = turns(gate_len)
+    gate_turns = gate_turns + jnp.where((lane & BINS) != 0, 0.25, 0.0)
+    table = cos_turns(gate_turns) * sums[:, :LANES] + cos_turns(gate_turns - 0.25) * sums[:, LANES:]
+    return (table * (1.0 / math.sqrt(taps * gate_len))).astype(jnp.bfloat16)
+
+
+def steer_rows(elem_x, elem_y, points, gate_len, quarter, store):
+    middle = gate_len // 12 + BINS // 2
+    distance = jnp.sqrt(
+        (elem_x - points[0]) ** 2 + (elem_y - points[1]) ** 2 + points[2] ** 2
+    )
+    turns = distance * (samples_per_mm / gate_len)
+    twice = 2.0 * cos_turns(turns)
+    for kind in range(2):
+        back = 0.25 * kind
+        now = cos_turns(turns * middle - back)
+        before = cos_turns(turns * (middle - 1) - back)
+        store(kind, BINS // 2, now)
+        store(kind, BINS // 2 - 1, before)
+        low, high = before, now
+        for f in range(BINS // 2 - 2, -1, -1):
+            low, high = twice * low - high, low
+            store(kind, f, low)
+        low, high = before, now
+        for f in range(BINS // 2 + 1, BINS):
+            low, high = high, twice * high - low
+            store(kind, f, high)
+
+
+def kernel(
+    tx_count,
+    rx_count,
+    cap_any,
+    grid_any,
+    exc_any,
+    vox_any,
+    out_ref,
+    cap,
+    grid,
+    exc,
+    vox,
+    steer_rx,
+    steer_tx,
+    send_spec,
+    recv_spec,
+    send_part,
+    recv_part,
+    load_sems,
+    spec_sems,
+    part_sems,
+):
+    devices = tx_count * rx_count
+    tx_rows, rx_cols, gate_len = cap.shape
+    subrun = rx_cols // tx_count
+    channels = 2 * BINS
+    width = subrun * subrun * channels
+    voxel_count = vox.shape[1]
+    owned = voxel_count // devices
+    me_tx, me_rx = lax.axis_index("tx"), lax.axis_index("rx")
+    me = me_tx * rx_count + me_rx
+    slot = me_rx * tx_count + me_tx
+
+    loads = [
+        pltpu.make_async_copy(source, target, load_sems.at[i])
+        for i, (source, target) in enumerate(
+            ((exc_any, exc), (cap_any, cap), (grid_any, grid), (vox_any, vox))
+        )
+    ]
+    for load in loads:
+        load.start()
+
+    def partner(i):
+        other = lax.rem(me + i, devices)
+        return other, lax.div(other, rx_count), lax.rem(other, rx_count)
+
+    barrier = pltpu.get_barrier_semaphore()
+
+    @pl.loop(1, devices)
+    def _(i):
+        _, tx, rx = partner(i)
+        pl.semaphore_signal(
+            barrier, inc=1, device_id=(tx, rx), device_id_type=pl.DeviceIdType.MESH
+        )
+
+    loads[0].wait()
+    table = filter_lanes(exc[...], gate_len)
+    table = jnp.concatenate([table] * (width // LANES), axis=1)
+    loads[1].wait()
+    group = iota((rx_cols, width), 1) // channels
+    inner = iota((rx_cols, width), 0) & (subrun - 1)
+    own_key = group - inner
+    sent_key = group - subrun * inner
+    rows = []
+    for t in range(tx_rows):
+        spec = matmul(cap[t], table)
+        own = jnp.where(own_key == subrun * (t % subrun), spec, 0.0)
+        sent = jnp.where(sent_key == t % subrun, spec, 0.0)
+        rows.append(jnp.concatenate([own, sent], axis=1).astype(jnp.bfloat16))
+    rows = jnp.concatenate(rows, axis=0)
+    pairs = tx_rows * rx_cols
+    pair = iota((devices, pairs), 1)
+    partner_row = (pair // (rx_cols * subrun)) * tx_count + (pair & (rx_cols - 1)) // subrun
+    both = matmul(one_hot(partner_row == iota((devices, pairs), 0)), rows)
+    own_spec = both[:, :width]
+    send_spec[...] = both[:, width:].reshape(devices, 1, width)
+    recv_spec[pl.ds(slot, 1)] = send_spec[pl.ds(slot, 1)]
+
+    pl.semaphore_wait(barrier, devices - 1)
+
+    @pl.loop(1, devices)
+    def _(i):
+        _, tx, rx = partner(i)
+        pltpu.make_async_remote_copy(
+            src_ref=send_spec.at[rx * tx_count + tx],
+            dst_ref=recv_spec.at[slot],
+            send_sem=spec_sems.at[0],
+            recv_sem=spec_sems.at[1],
+            device_id=(tx, rx),
+            device_id_type=pl.DeviceIdType.MESH,
+        ).start()
+
+    loads[2].wait()
+    loads[3].wait()
+    elements = grid.shape[1]
+    cells = grid[...].astype(jnp.float32)
+    x_line = (cells[0:1] - 0.5 * (elements // 32 - 1)) * pitch_mm
+    y_line = (cells[1:2] - 15.5) * pitch_mm
+    points = voxel_points(vox[...])
+    points = tuple(p.reshape(1, voxel_count) for p in points)
+
+    def columns(chosen):
+        return (
+            jnp.sum(jnp.where(chosen, x_line, 0.0), axis=1, keepdims=True),
+            jnp.sum(jnp.where(chosen, y_line, 0.0), axis=1, keepdims=True),
+        )
+
+    chunk = 16
+    for first in range(0, rx_cols, chunk):
+        j = iota((chunk, elements), 0) + first
+        element = (j // subrun) * tx_rows + me_rx * subrun + (j & (subrun - 1))
+        elem_x, elem_y = columns(iota((chunk, elements), 1) == element)
+
+        def store(kind, f, values, first=first):
+            steer_rx[f, pl.ds(kind * rx_cols + first, chunk), :] = values.astype(jnp.bfloat16)
+
+        steer_rows(elem_x, elem_y, points, gate_len, 0, store)
+    element = iota((tx_rows, elements), 0) + me_tx * tx_rows
+    elem_x, elem_y = columns(iota((tx_rows, elements), 1) == element)
+
+    def store_tx(kind, f, values):
+        steer_tx[f, pl.ds(kind * tx_rows, tx_rows), :] = values
+
+    steer_rows(elem_x, elem_y, points, gate_len, 0, store_tx)
+
+    same = one_hot(iota((width, width), 0) // channels == iota((width, width), 1) // channels)
+    spread_rows = 2 * rx_cols
+    spread = one_hot(
+        iota((spread_rows, 2 * tx_count), 0) // subrun == iota((spread_rows, 2 * tx_count), 1)
+    )
+    long = rx_count * width
+    kept = (iota((spread_rows, long), 1) // channels) % subrun == (
+        iota((spread_rows, long), 0) & (subrun - 1)
+    )
+    fold_row = iota((channels * tx_rows, long), 0)
+    fold_lane = iota((channels * tx_rows, long), 1)
+    fold = one_hot(
+        ((fold_row & (tx_rows - 1)) == fold_lane // (subrun * channels))
+        & (fold_row // tx_rows == (fold_lane & (BINS - 1)) * 2 + ((fold_lane // BINS) & 1))
+    )
+
+    pltpu.make_async_copy(
+        recv_spec.at[pl.ds(0, devices - 1)], recv_spec.at[pl.ds(0, devices - 1)], spec_sems.at[1]
+    ).wait()
+    averaged = (own_spec + recv_spec[...].reshape(devices, width)) * 0.5
+    square = averaged * averaged
+    high = square.astype(jnp.bfloat16)
+    low = (square - high.astype(jnp.float32)).astype(jnp.bfloat16)
+    power = (matmul(high, same) + matmul(low, same)) * (1.0 / channels)
+    whitened = averaged * lax.rsqrt(jnp.maximum(power, power_floor))
+    imag_lane = (iota((devices, width), 1) & BINS) != 0
+    turned = jnp.where(
+        imag_lane, pltpu.roll(whitened, BINS, 1), -pltpu.roll(whitened, width - BINS, 1)
+    )
+
+    def side(values):
+        return jnp.concatenate(
+            [values[b * tx_count : (b + 1) * tx_count] for b in range(rx_count)], axis=1
+        )
+
+    both = jnp.concatenate([side(whitened), side(turned)], axis=0).astype(jnp.bfloat16)
+    wide = jnp.where(kept, matmul(spread, both), 0.0).astype(jnp.bfloat16)
+    left = lax.dot_general(
+        fold, wide, (((1,), (1,)), ((), ())), preferred_element_type=jnp.float32
+    ).astype(jnp.bfloat16)
+    real = jnp.zeros((tx_rows, voxel_count), jnp.float32)
+    imag = jnp.zeros((tx_rows, voxel_count), jnp.float32)
+    for f in range(BINS):
+        products = matmul(left[2 * tx_rows * f : 2 * tx_rows * (f + 1)], steer_rx[f])
+        prod_real, prod_imag = products[:tx_rows], products[tx_rows:]
+        tx_cosine, tx_sine = steer_tx[f, :tx_rows, :], steer_tx[f, tx_rows:, :]
+        real += prod_real * tx_cosine - prod_imag * tx_sine
+        imag += prod_real * tx_sine + prod_imag * tx_cosine
+    image = jnp.concatenate(
+        [jnp.sum(real, axis=0, keepdims=True), jnp.sum(imag, axis=0, keepdims=True)], axis=0
+    ) * (1.0 / (elements * math.sqrt(BINS)))
+    for tile in range(voxel_count // LANES):
+        send_part[tile] = image[:, tile * LANES : (tile + 1) * LANES]
+    per_tile = LANES // owned
+
+    @pl.loop(1, devices)
+    def _(i):
+        other, tx, rx = partner(i)
+        pltpu.make_async_remote_copy(
+            src_ref=send_part.at[lax.div(other, per_tile)],
+            dst_ref=recv_part.at[me],
+            send_sem=part_sems.at[0],
+            recv_sem=part_sems.at[1],
+            device_id=(tx, rx),
+            device_id_type=pl.DeviceIdType.MESH,
+        ).start()
+
+    recv_part[pl.ds(me, 1)] = send_part[pl.ds(lax.div(me, per_tile), 1)]
+    all_but_one = recv_part.at[pl.ds(0, devices - 1)]
+    pltpu.make_async_copy(all_but_one, all_but_one, part_sems.at[1]).wait()
+    total = jnp.sum(recv_part[...], axis=0)
+    shift = lax.rem(LANES - owned * lax.rem(me, per_tile), LANES)
+    out_ref[...] = pltpu.roll(total, shift, 1)[:, :owned]
+    sent_spec = send_spec.at[pl.ds(0, devices - 1)]
+    pltpu.make_async_copy(sent_spec, sent_spec, spec_sems.at[0]).wait()
+    pltpu.make_async_copy(all_but_one, all_but_one, part_sems.at[0]).wait()
+
+
+def small(captures, elem_grid, excitation, voxels):
+    tx_count = lax.axis_size("tx")
+    rx_count = lax.axis_size("rx")
+    devices = tx_count * rx_count
+    tx_rows, rx_cols, gate_len = captures.shape
+    voxel_count = voxels.shape[1]
+    width = (rx_cols // tx_count) ** 2 * 2 * BINS
+    excitation = excitation.reshape(1, -1)
+    return pl.pallas_call(
+        functools.partial(kernel, tx_count, rx_count),
+        out_shape=jax.ShapeDtypeStruct((2, voxel_count // devices), jnp.float32),
+        in_specs=[pl.BlockSpec(memory_space=pl.ANY)] * 4,
+        out_specs=pl.BlockSpec(memory_space=pltpu.VMEM),
+        scratch_shapes=[
+            pltpu.VMEM(captures.shape, captures.dtype),
+            pltpu.VMEM(elem_grid.shape, jnp.int32),
+            pltpu.VMEM(excitation.shape, jnp.int32),
+            pltpu.VMEM(voxels.shape, jnp.int32),
+            pltpu.VMEM((BINS, 2 * rx_cols, voxel_count), jnp.bfloat16),
+            pltpu.VMEM((BINS, 2 * tx_rows, voxel_count), jnp.float32),
+            pltpu.VMEM((devices, 1, width), jnp.float32),
+            pltpu.VMEM((devices, 1, width), jnp.float32),
+            pltpu.VMEM((voxel_count // LANES, 2, LANES), jnp.float32),
+            pltpu.VMEM((devices, 2, LANES), jnp.float32),
+            pltpu.SemaphoreType.DMA((4,)),
+            pltpu.SemaphoreType.DMA((2,)),
+            pltpu.SemaphoreType.DMA((2,)),
+        ],
+        compiler_params=pltpu.CompilerParams(
+            collective_id=0, has_side_effects=True, vmem_limit_bytes=32 * 1024 * 1024
+        ),
+    )(captures, elem_grid, excitation, voxels)
+
+
+def local(captures, elem_grid, excitation, voxels):
+    tx_count = lax.axis_size("tx")
+    devices = tx_count * lax.axis_size("rx")
+    tx_rows, rx_cols, _ = captures.shape
+    fits = (
+        tx_rows == 8
+        and rx_cols == 64
+        and rx_cols // tx_count == 4
+        and voxels.shape[1] <= 1024
+        and LANES % (voxels.shape[1] // devices) == 0
+    )
+    return (small if fits else general)(captures, elem_grid, excitation, voxels)
+
+
 def solution(mesh):
     placed = (P("tx", "rx", None), P(), P(), P())
     return jax.shard_map(

time: 179 us -> 20.1 us (0.11)
  waiting for transfers between devices: 135 us -> 0 us
  Pallas kernels: 0 us -> 17 us
  between operations: 13.6 us -> 0.01 us
  other arithmetic: 11.2 us -> 0 us
  starting transfers between devices: 8.35 us -> 0 us
  blocking collectives: 3.94 us -> 0 us
  local copies, waits for them, and re-layouts: 5.04 us -> 2.9 us
    unnamed x2 -> x0, waiting for transfers between devices: 135 us -> none
    pallas_call x0 -> x1, Pallas kernels: none -> 17 us  [small(): pl.pallas_call(functools.partial(kernel, tx_count, rx_count), out_shape=j...]
    all_to_all x1 -> x0, starting transfers between devices: 8.31 us -> none  [local(): lax.all_to_all(pieces, 'tx', split_axis=2, concat_axis=2, tiled=True)]
    convert_element_type x4 -> x0, other arithmetic: 4.15 us -> none  [the longest x1 4.05 us: image_block(): rx_sine = jnp.sin(recv_phase).astype(jnp.bfloat16)]
    all_to_all x1 -> x0, blocking collectives: 3.94 us -> none  [local(): lax.all_to_all(lax.all_to_all(pieces, 'tx', split_axis=2, concat_axis=2,...]
    neg x1 -> x0, other arithmetic: 3.63 us -> none  [image_block(): -rx_sine]
    reduce_sum x2 -> x0, other arithmetic: 3.04 us -> none  [the longest x1 2.45 us: filter_table(): real_part = jnp.sum(weight * jnp.cos(phases), axis=1) * norm_scale]
    reshape x4 -> x0, local copies, waits for them, and re-layouts: 2.07 us -> none  [the longest x2 1.83 us: local(): pieces = captures.reshape(rx_count, subrun, tx_count, subrun, gate_len)]
  transfers between devices with their start and end apart: 2 -> 0, of which waited for: 1 -> 0; matrix products, arithmetic and copies ran while one was open for 6% -> 0% of each run, Pallas kernels for 0% -> 0%
where the time goes in v1:
time: 20.1 us; the launch traced here: 19.9 us
  Pallas kernels  17 us (85%)
  local copies, waits for them, and re-layouts  2.9 us (14%)
    pallas_call x1, Pallas kernels, small(): pl.pallas_call(functools.partial(kernel, tx_count, rx_count), out_shape=j...  17 us
    unnamed x9, local copies, waits for them, and re-layouts  2.9 us

profile of v1, /device:TPU:0, one launch (start us, length us, event | category | flops | bytes accessed | tf_op | source)
XLA Modules:
  0.0 19.9 jit_solution(16580152770270818580)
XLA Ops:
  0.0 0.0 copy-start.3
  0.0 0.0 copy-start.2
  0.0 0.7 %copy-done.3 = s32[64]{0:T(128)S(1)} copy-done((s32[64]{0:T(128)S(1)}, s32[64]{0:T(128)}, u32[]{:S(2)}) %copy-start.3) | copy-done | bytes 280
  0.7 0.0 copy-done.2
  0.7 0.0 copy-start
  0.7 0.9 %copy-done = bf16[8,64,256]{2,1,0:T(8,128)(2,1)S(1)} copy-done((bf16[8,64,256]{2,1,0:T(8,128)(2,1)S(1)}, bf16[8,64,256]{2,1,0:T(8,128)(2,1)}, u32[]{:S(2)}) %copy-start) | copy-done | bytes 262168
  1.6 0.0 copy-start.1
  1.6 0.7 %copy-done.1 = s32[3,512]{1,0:T(4,128)S(1)} copy-done((s32[3,512]{1,0:T(4,128)S(1)}, s32[3,512]{1,0:T(4,128)}, u32[]{:S(2)}) %copy-start.1) | copy-done | bytes 6168
  2.3 17.0 %shard_map.46 = f32[2,16]{1,0:T(2,128)S(1)} custom-call(bf16[8,64,256]{2,1,0:T(8,128)(2,1)S(1)} %copy-done, s32[2,128]{1,0:T(2,128)S(1)} %copy-done.2, s32[1,64]{1,0:T(1,128)S(1)} %bitcast.1, s32[3,512]{1,0:T(4,128)S(1)} %copy-done.1), custom_call_target="tpu_custom_call" | custom-call | tf_op jit(solution)/shard_map/pallas_call | solution.py:431
  19.3 0.6 %copy.6 = f32[2,16]{1,0:T(2,128)} copy(f32[2,16]{1,0:T(2,128)S(1)} %shard_map.46) | data formatting | bytes 256
Async XLA Ops:
  0.0 0.7 %copy-start.3 = (s32[64]{0:T(128)S(1)}, s32[64]{0:T(128)}, u32[]{:S(2)}) copy-start(s32[64]{0:T(128)} %param.6) | copy-start | bytes 772
  0.0 0.7 %copy-start.2 = (s32[2,128]{1,0:T(2,128)S(1)}, s32[2,128]{1,0:T(2,128)}, u32[]{:S(2)}) copy-start(s32[2,128]{1,0:T(2,128)} %grid_any.1) | copy-start | bytes 3076
  0.7 0.9 %copy-start = (bf16[8,64,256]{2,1,0:T(8,128)(2,1)S(1)}, bf16[8,64,256]{2,1,0:T(8,128)(2,1)}, u32[]{:S(2)}) copy-start(bf16[8,64,256]{2,1,0:T(8,128)(2,1)} %cap_any.1) | copy-start | bytes 786436
  1.6 0.7 %copy-start.1 = (s32[3,512]{1,0:T(4,128)S(1)}, s32[3,512]{1,0:T(4,128)}, u32[]{:S(2)}) copy-start(s32[3,512]{1,0:T(4,128)} %vox_any.1) | copy-start | bytes 18436

commit v2 on v1

--- a/solution.py
+++ b/solution.py
@@ -170,8 +170,7 @@
     return jnp.dot(left, right, preferred_element_type=jnp.float32)
 
 
-def filter_lanes(excitation, gate_len):
-    taps = excitation.shape[1]
+def filter_lanes(taps, gate_len):
     first_bin = gate_len // 12
 
     def turns(rows):
@@ -186,12 +185,18 @@
     middle = rest.astype(jnp.bfloat16)
     low = (rest - middle.astype(jnp.float32)).astype(jnp.bfloat16)
     reached = iota((gate_len, taps), 1) <= iota((gate_len, taps), 0)
-    weight = jnp.where(reached, excitation.astype(jnp.float32), 0.0).astype(jnp.bfloat16)
-    sums = matmul(weight, high) + (matmul(weight, middle) + matmul(weight, low))
     gate_turns, lane = turns(gate_len)
     gate_turns = gate_turns + jnp.where((lane & BINS) != 0, 0.25, 0.0)
-    table = cos_turns(gate_turns) * sums[:, :LANES] + cos_turns(gate_turns - 0.25) * sums[:, LANES:]
-    return (table * (1.0 / math.sqrt(taps * gate_len))).astype(jnp.bfloat16)
+    scale = 1.0 / math.sqrt(taps * gate_len)
+    by_cosine = cos_turns(gate_turns) * scale
+    by_sine = cos_turns(gate_turns - 0.25) * scale
+
+    def table(excitation):
+        weight = jnp.where(reached, excitation.astype(jnp.float32), 0.0).astype(jnp.bfloat16)
+        sums = matmul(weight, high) + (matmul(weight, middle) + matmul(weight, low))
+        return (by_cosine * sums[:, :LANES] + by_sine * sums[:, LANES:]).astype(jnp.bfloat16)
+
+    return table
 
 
 def steer_rows(elem_x, elem_y, points, gate_len, quarter, store):
@@ -259,27 +264,38 @@
     for load in loads:
         load.start()
 
-    def partner(i):
-        other = lax.rem(me + i, devices)
-        return other, lax.div(other, rx_count), lax.rem(other, rx_count)
+    def place(other):
+        return lax.div(other, rx_count), lax.rem(other, rx_count)
+
+    def wait_rows(ref, semaphore, count):
+        for rows in range(1, devices):
+
+            @pl.when(count == rows)
+            def _(rows=rows):
+                some = ref.at[pl.ds(0, rows)]
+                pltpu.make_async_copy(some, some, semaphore).wait()
 
     barrier = pltpu.get_barrier_semaphore()
 
-    @pl.loop(1, devices)
-    def _(i):
-        _, tx, rx = partner(i)
+    @pl.loop(me + 1, devices)
+    def _(other):
         pl.semaphore_signal(
-            barrier, inc=1, device_id=(tx, rx), device_id_type=pl.DeviceIdType.MESH
-        )
-
-    loads[0].wait()
-    table = filter_lanes(exc[...], gate_len)
-    table = jnp.concatenate([table] * (width // LANES), axis=1)
-    loads[1].wait()
+            barrier, inc=1, device_id=place(other), device_id_type=pl.DeviceIdType.MESH
+        )
+
+    make_table = filter_lanes(exc.shape[1], gate_len)
     group = iota((rx_cols, width), 1) // channels
     inner = iota((rx_cols, width), 0) & (subrun - 1)
     own_key = group - inner
     sent_key = group - subrun * inner
+    pairs = tx_rows * rx_cols
+    pair = iota((devices, pairs), 1)
+    partner_row = (pair // (rx_cols * subrun)) * tx_count + (pair & (rx_cols - 1)) // subrun
+    gather = one_hot(partner_row == iota((devices, pairs), 0))
+    loads[0].wait()
+    table = make_table(exc[...])
+    table = jnp.concatenate([table] * (width // LANES), axis=1)
+    loads[1].wait()
     rows = []
     for t in range(tx_rows):
         spec = matmul(cap[t], table)
@@ -287,19 +303,18 @@
         sent = jnp.where(sent_key == t % subrun, spec, 0.0)
         rows.append(jnp.concatenate([own, sent], axis=1).astype(jnp.bfloat16))
     rows = jnp.concatenate(rows, axis=0)
-    pairs = tx_rows * rx_cols
-    pair = iota((devices, pairs), 1)
-    partner_row = (pair // (rx_cols * subrun)) * tx_count + (pair & (rx_cols - 1)) // subrun
-    both = matmul(one_hot(partner_row == iota((devices, pairs), 0)), rows)
+    both = matmul(gather, rows)
     own_spec = both[:, :width]
     send_spec[...] = both[:, width:].reshape(devices, 1, width)
     recv_spec[pl.ds(slot, 1)] = send_spec[pl.ds(slot, 1)]
 
-    pl.semaphore_wait(barrier, devices - 1)
-
-    @pl.loop(1, devices)
-    def _(i):
-        _, tx, rx = partner(i)
+    @pl.when(me > 0)
+    def _():
+        pl.semaphore_wait(barrier, me)
+
+    @pl.loop(0, me)
+    def _(other):
+        tx, rx = place(other)
         pltpu.make_async_remote_copy(
             src_ref=send_spec.at[rx * tx_count + tx],
             dst_ref=recv_spec.at[slot],
@@ -358,16 +373,19 @@
         & (fold_row // tx_rows == (fold_lane & (BINS - 1)) * 2 + ((fold_lane // BINS) & 1))
     )
 
-    pltpu.make_async_copy(
-        recv_spec.at[pl.ds(0, devices - 1)], recv_spec.at[pl.ds(0, devices - 1)], spec_sems.at[1]
-    ).wait()
-    averaged = (own_spec + recv_spec[...].reshape(devices, width)) * 0.5
+    row = iota((devices, width), 0)
+    sender = lax.rem(row, tx_count) * rx_count + lax.div(row, tx_count)
+    times = jnp.where(sender > me, 2.0, 1.0)
+    used = sender >= me
+    imag_lane = (iota((devices, width), 1) & BINS) != 0
+
+    wait_rows(recv_spec, spec_sems.at[1], devices - 1 - me)
+    averaged = jnp.where(used, own_spec + recv_spec[...].reshape(devices, width), 0.0) * 0.5
     square = averaged * averaged
     high = square.astype(jnp.bfloat16)
     low = (square - high.astype(jnp.float32)).astype(jnp.bfloat16)
     power = (matmul(high, same) + matmul(low, same)) * (1.0 / channels)
-    whitened = averaged * lax.rsqrt(jnp.maximum(power, power_floor))
-    imag_lane = (iota((devices, width), 1) & BINS) != 0
+    whitened = averaged * lax.rsqrt(jnp.maximum(power, power_floor)) * times
     turned = jnp.where(
         imag_lane, pltpu.roll(whitened, BINS, 1), -pltpu.roll(whitened, width - BINS, 1)
     )
@@ -397,9 +415,10 @@
         send_part[tile] = image[:, tile * LANES : (tile + 1) * LANES]
     per_tile = LANES // owned
 
-    @pl.loop(1, devices)
+    @pl.loop(0, devices - 1)
     def _(i):
-        other, tx, rx = partner(i)
+        other = i + jnp.where(i >= me, 1, 0)
+        tx, rx = place(other)
         pltpu.make_async_remote_copy(
             src_ref=send_part.at[lax.div(other, per_tile)],
             dst_ref=recv_part.at[me],
@@ -415,8 +434,7 @@
     total = jnp.sum(recv_part[...], axis=0)
     shift = lax.rem(LANES - owned * lax.rem(me, per_tile), LANES)
     out_ref[...] = pltpu.roll(total, shift, 1)[:, :owned]
-    sent_spec = send_spec.at[pl.ds(0, devices - 1)]
-    pltpu.make_async_copy(sent_spec, sent_spec, spec_sems.at[0]).wait()
+    wait_rows(send_spec, spec_sems.at[0], me)
     pltpu.make_async_copy(all_but_one, all_but_one, part_sems.at[0]).wait()
 
 
@@ -431,7 +449,7 @@
     return pl.pallas_call(
         functools.partial(kernel, tx_count, rx_count),
         out_shape=jax.ShapeDtypeStruct((2, voxel_count // devices), jnp.float32),
-        in_specs=[pl.BlockSpec(memory_space=pl.ANY)] * 4,
+        in_specs=[pl.BlockSpec(memory_space=pltpu.HBM)] * 4,
         out_specs=pl.BlockSpec(memory_space=pltpu.VMEM),
         scratch_shapes=[
             pltpu.VMEM(captures.shape, captures.dtype),
@@ -449,7 +467,7 @@
             pltpu.SemaphoreType.DMA((2,)),
         ],
         compiler_params=pltpu.CompilerParams(
-            collective_id=0, has_side_effects=True, vmem_limit_bytes=32 * 1024 * 1024
+            collective_id=0, has_side_effects=True
         ),
     )(captures, elem_grid, excitation, voxels)
 

time: 20.1 us -> 16.1 us (0.80)
  Pallas kernels: 17 us -> 14.7 us
  local copies, waits for them, and re-layouts: 2.9 us -> 1.24 us
    pallas_call x1, Pallas kernels: 17 us -> 14.7 us  [small(): pl.pallas_call(functools.partial(kernel, tx_count, rx_count), out_shape=j...]
    unnamed x9 -> x1, local copies, waits for them, and re-layouts: 2.9 us -> 1.24 us
where the time goes in v2:
time: 16.1 us; the launch traced here: 15.9 us
  Pallas kernels  14.7 us (91%)
  local copies, waits for them, and re-layouts  1.24 us (8%)
    pallas_call x1, Pallas kernels, small(): pl.pallas_call(functools.partial(kernel, tx_count, rx_count), out_shape=j...  14.7 us
    unnamed x1, local copies, waits for them, and re-layouts  1.24 us

profile of v2, /device:TPU:0, one launch (start us, length us, event | category | flops | bytes accessed | tf_op | source)
XLA Modules:
  0.0 15.9 jit_solution(3885814092335029082)
XLA Ops:
  0.0 14.7 %shard_map.46 = f32[2,16]{1,0:T(2,128)} custom-call(bf16[8,64,256]{2,1,0:T(8,128)(2,1)} %cap_any.1, s32[2,128]{1,0:T(2,128)} %grid_any.1, s32[1,64]{1,0:T(1,128)} %bitcast.1, s32[3,512]{1,0:T(4,128)} %vox_any.1), custom_call_target="tpu_custom_call" | custom-call | tf_op jit(solution)/shard_map/pallas_call | solution.py:449
  14.7 1.2 %copy.6 = f32[2,16]{1,0:T(2,128)} copy(f32[2,16]{1,0:T(2,128)} %shard_map.46) | data formatting | bytes 256

commit v3 on v2

--- a/solution.py
+++ b/solution.py
@@ -446,9 +446,13 @@
     voxel_count = voxels.shape[1]
     width = (rx_cols // tx_count) ** 2 * 2 * BINS
     excitation = excitation.reshape(1, -1)
+    operands = [
+        pltpu.with_memory_space_constraint(x, pltpu.HBM)
+        for x in (captures, elem_grid, excitation, voxels)
+    ]
     return pl.pallas_call(
         functools.partial(kernel, tx_count, rx_count),
-        out_shape=jax.ShapeDtypeStruct((2, voxel_count // devices), jnp.float32),
+        out_shape=pltpu.VMEM((2, voxel_count // devices), jnp.float32),
         in_specs=[pl.BlockSpec(memory_space=pltpu.HBM)] * 4,
         out_specs=pl.BlockSpec(memory_space=pltpu.VMEM),
         scratch_shapes=[
@@ -467,9 +471,9 @@
             pltpu.SemaphoreType.DMA((2,)),
         ],
         compiler_params=pltpu.CompilerParams(
-            collective_id=0, has_side_effects=True
+            collective_id=0, has_side_effects=True, vmem_limit_bytes=32 * 1024 * 1024
         ),
-    )(captures, elem_grid, excitation, voxels)
+    )(*operands)
 
 
 def local(captures, elem_grid, excitation, voxels):

time: 16.1 us -> 14.8 us (0.919)
  local copies, waits for them, and re-layouts: 1.24 us -> 0.56 us
  Pallas kernels: 14.7 us -> 14.1 us
    unnamed x1, local copies, waits for them, and re-layouts: 1.24 us -> 0.56 us
    pallas_call x1, Pallas kernels: 14.7 us -> 14.1 us  [small(): pl.pallas_call(functools.partial(kernel, tx_count, rx_count), out_shape=p...]
where the time goes in v3:
time: 14.8 us; the launch traced here: 14.7 us
  Pallas kernels  14.1 us (95%)
  local copies, waits for them, and re-layouts  0.56 us (4%)
    pallas_call x1, Pallas kernels, small(): pl.pallas_call(functools.partial(kernel, tx_count, rx_count), out_shape=p...  14.1 us
    unnamed x1, local copies, waits for them, and re-layouts  0.56 us

profile of v3, /device:TPU:0, one launch (start us, length us, event | category | flops | bytes accessed | tf_op | source)
XLA Modules:
  0.0 14.7 jit_solution(1358327372006692080)
XLA Ops:
  0.0 14.1 %shard_map.46 = f32[2,16]{1,0:T(2,128)S(1)} custom-call(bf16[8,64,256]{2,1,0:T(8,128)(2,1)} %cap_any.1, s32[2,128]{1,0:T(2,128)} %grid_any.1, s32[1,64]{1,0:T(1,128)} %bitcast.1, s32[3,512]{1,0:T(4,128)} %vox_any.1), custom_call_target="tpu_custom_call" | custom-call | tf_op jit(solution)/shard_map/pallas_call | solution.py:453
  14.1 0.6 %copy.6 = f32[2,16]{1,0:T(2,128)} copy(f32[2,16]{1,0:T(2,128)S(1)} %shard_map.46) | data formatting | bytes 256

commit v4 on v3

--- a/solution.py
+++ b/solution.py
@@ -255,11 +255,12 @@
     me = me_tx * rx_count + me_rx
     slot = me_rx * tx_count + me_tx
 
+    halves = [pl.ds(b * subrun, subrun) for b in range(rx_count)]
+    pieces = [(cap_any.at[half], cap.at[half]) for half in halves]
+    pieces += [(exc_any, exc), (grid_any, grid), (vox_any, vox)]
     loads = [
         pltpu.make_async_copy(source, target, load_sems.at[i])
-        for i, (source, target) in enumerate(
-            ((exc_any, exc), (cap_any, cap), (grid_any, grid), (vox_any, vox))
-        )
+        for i, (source, target) in enumerate(pieces)
     ]
     for load in loads:
         load.start()
@@ -267,13 +268,17 @@
     def place(other):
         return lax.div(other, rx_count), lax.rem(other, rx_count)
 
-    def wait_rows(ref, semaphore, count):
-        for rows in range(1, devices):
-
-            @pl.when(count == rows)
-            def _(rows=rows):
-                some = ref.at[pl.ds(0, rows)]
-                pltpu.make_async_copy(some, some, semaphore).wait()
+    def wait_rows(ref, semaphore, count, low=0, high=devices):
+        if high - low > 1:
+            middle = (low + high) // 2
+            for side, span in ((count < middle, (low, middle)), (count >= middle, (middle, high))):
+
+                @pl.when(side)
+                def _(span=span):
+                    wait_rows(ref, semaphore, count, *span)
+        elif low:
+            some = ref.at[pl.ds(0, low)]
+            pltpu.make_async_copy(some, some, semaphore).wait()
 
     barrier = pltpu.get_barrier_semaphore()
 
@@ -284,28 +289,26 @@
         )
 
     make_table = filter_lanes(exc.shape[1], gate_len)
-    group = iota((rx_cols, width), 1) // channels
-    inner = iota((rx_cols, width), 0) & (subrun - 1)
-    own_key = group - inner
-    sent_key = group - subrun * inner
-    pairs = tx_rows * rx_cols
-    pair = iota((devices, pairs), 1)
-    partner_row = (pair // (rx_cols * subrun)) * tx_count + (pair & (rx_cols - 1)) // subrun
-    gather = one_hot(partner_row == iota((devices, pairs), 0))
-    loads[0].wait()
+    pairs = subrun * rx_cols
+    group = iota((pairs, width), 1) // channels
+    outer = iota((pairs, width), 0) // rx_cols
+    inner = iota((pairs, width), 0) & (subrun - 1)
+    own_kept = group == subrun * outer + inner
+    sent_kept = group == subrun * inner + outer
+    pair = iota((tx_count, pairs), 1)
+    gather = one_hot((pair & (rx_cols - 1)) // subrun == iota((tx_count, pairs), 0))
+    loads[rx_count].wait()
     table = make_table(exc[...])
     table = jnp.concatenate([table] * (width // LANES), axis=1)
-    loads[1].wait()
-    rows = []
-    for t in range(tx_rows):
-        spec = matmul(cap[t], table)
-        own = jnp.where(own_key == subrun * (t % subrun), spec, 0.0)
-        sent = jnp.where(sent_key == t % subrun, spec, 0.0)
-        rows.append(jnp.concatenate([own, sent], axis=1).astype(jnp.bfloat16))
-    rows = jnp.concatenate(rows, axis=0)
-    both = matmul(gather, rows)
-    own_spec = both[:, :width]
-    send_spec[...] = both[:, width:].reshape(devices, 1, width)
+    own_spec = []
+    for b in range(rx_count):
+        loads[b].wait()
+        spec = matmul(cap[halves[b]].reshape(pairs, gate_len), table)
+        kept = [jnp.where(mask, spec, 0.0) for mask in (own_kept, sent_kept)]
+        both = matmul(gather, jnp.concatenate(kept, axis=1).astype(jnp.bfloat16))
+        own_spec.append(both[:, :width])
+        send_spec[pl.ds(b * tx_count, tx_count)] = both[:, width:].reshape(tx_count, 1, width)
+    own_spec = jnp.concatenate(own_spec, axis=0)
     recv_spec[pl.ds(slot, 1)] = send_spec[pl.ds(slot, 1)]
 
     @pl.when(me > 0)
@@ -324,8 +327,8 @@
             device_id_type=pl.DeviceIdType.MESH,
         ).start()
 
-    loads[2].wait()
-    loads[3].wait()
+    loads[rx_count + 1].wait()
+    loads[rx_count + 2].wait()
     elements = grid.shape[1]
     cells = grid[...].astype(jnp.float32)
     x_line = (cells[0:1] - 0.5 * (elements // 32 - 1)) * pitch_mm
@@ -400,42 +403,51 @@
     left = lax.dot_general(
         fold, wide, (((1,), (1,)), ((), ())), preferred_element_type=jnp.float32
     ).astype(jnp.bfloat16)
-    real = jnp.zeros((tx_rows, voxel_count), jnp.float32)
-    imag = jnp.zeros((tx_rows, voxel_count), jnp.float32)
-    for f in range(BINS):
-        products = matmul(left[2 * tx_rows * f : 2 * tx_rows * (f + 1)], steer_rx[f])
-        prod_real, prod_imag = products[:tx_rows], products[tx_rows:]
-        tx_cosine, tx_sine = steer_tx[f, :tx_rows, :], steer_tx[f, tx_rows:, :]
-        real += prod_real * tx_cosine - prod_imag * tx_sine
-        imag += prod_real * tx_sine + prod_imag * tx_cosine
-    image = jnp.concatenate(
-        [jnp.sum(real, axis=0, keepdims=True), jnp.sum(imag, axis=0, keepdims=True)], axis=0
-    ) * (1.0 / (elements * math.sqrt(BINS)))
-    for tile in range(voxel_count // LANES):
-        send_part[tile] = image[:, tile * LANES : (tile + 1) * LANES]
     per_tile = LANES // owned
-
-    @pl.loop(0, devices - 1)
-    def _(i):
-        other = i + jnp.where(i >= me, 1, 0)
-        tx, rx = place(other)
-        pltpu.make_async_remote_copy(
-            src_ref=send_part.at[lax.div(other, per_tile)],
-            dst_ref=recv_part.at[me],
-            send_sem=part_sems.at[0],
-            recv_sem=part_sems.at[1],
-            device_id=(tx, rx),
-            device_id_type=pl.DeviceIdType.MESH,
-        ).start()
+    scale = 1.0 / (elements * math.sqrt(BINS))
+    tiles = voxel_count // LANES
+    for first, last in ((0, 1), (1, tiles)):
+        lanes = pl.ds(first * LANES, (last - first) * LANES)
+        real = jnp.zeros((tx_rows, (last - first) * LANES), jnp.float32)
+        imag = jnp.zeros_like(real)
+        for f in range(BINS):
+            products = matmul(
+                left[2 * tx_rows * f : 2 * tx_rows * (f + 1)], steer_rx[f, :, lanes]
+            )
+            prod_real, prod_imag = products[:tx_rows], products[tx_rows:]
+            tx_cosine = steer_tx[f, pl.ds(0, tx_rows), lanes]
+            tx_sine = steer_tx[f, pl.ds(tx_rows, tx_rows), lanes]
+            real += prod_real * tx_cosine - prod_imag * tx_sine
+            imag += prod_real * tx_sine + prod_imag * tx_cosine
+        image = jnp.concatenate(
+            [jnp.sum(real, axis=0, keepdims=True), jnp.sum(imag, axis=0, keepdims=True)], axis=0
+        )
+        image = image * scale
+        for tile in range(first, last):
+            begin = (tile - first) * LANES
+            send_part[tile] = image[:, begin : begin + LANES]
+
+        @pl.loop(first * per_tile, last * per_tile)
+        def _(other):
+            @pl.when(other != me)
+            def _():
+                pltpu.make_async_remote_copy(
+                    src_ref=send_part.at[lax.div(other, per_tile)],
+                    dst_ref=recv_part.at[me],
+                    send_sem=part_sems.at[0],
+                    recv_sem=part_sems.at[1],
+                    device_id=place(other),
+                    device_id_type=pl.DeviceIdType.MESH,
+                ).start()
 
     recv_part[pl.ds(me, 1)] = send_part[pl.ds(lax.div(me, per_tile), 1)]
     all_but_one = recv_part.at[pl.ds(0, devices - 1)]
-    pltpu.make_async_copy(all_but_one, all_but_one, part_sems.at[1]).wait()
+    wait_rows(send_spec, spec_sems.at[0], me)
+    for semaphore in range(2):
+        pltpu.make_async_copy(all_but_one, all_but_one, part_sems.at[semaphore]).wait()
     total = jnp.sum(recv_part[...], axis=0)
     shift = lax.rem(LANES - owned * lax.rem(me, per_tile), LANES)
     out_ref[...] = pltpu.roll(total, shift, 1)[:, :owned]
-    wait_rows(send_spec, spec_sems.at[0], me)
-    pltpu.make_async_copy(all_but_one, all_but_one, part_sems.at[0]).wait()
 
 
 def small(captures, elem_grid, excitation, voxels):
@@ -466,7 +478,7 @@
             pltpu.VMEM((devices, 1, width), jnp.float32),
             pltpu.VMEM((voxel_count // LANES, 2, LANES), jnp.float32),
             pltpu.VMEM((devices, 2, LANES), jnp.float32),
-            pltpu.SemaphoreType.DMA((4,)),
+            pltpu.SemaphoreType.DMA((rx_count + 3,)),
             pltpu.SemaphoreType.DMA((2,)),
             pltpu.SemaphoreType.DMA((2,)),
         ],

time: 14.8 us -> 14.8 us (level)
  no operation moved by 1% of the time
where the time goes in v4:
time: 14.8 us; the launch traced here: 14.6 us
  Pallas kernels  14 us (95%)
  local copies, waits for them, and re-layouts  0.56 us (4%)
    pallas_call x1, Pallas kernels, small(): pl.pallas_call(functools.partial(kernel, tx_count, rx_count), out_shape=p...  14 us
    unnamed x1, local copies, waits for them, and re-layouts  0.56 us

profile of v4, /device:TPU:0, one launch (start us, length us, event | category | flops | bytes accessed | tf_op | source)
XLA Modules:
  0.0 14.6 jit_solution(4252525131937589843)
XLA Ops:
  0.0 14.0 %shard_map.46 = f32[2,16]{1,0:T(2,128)S(1)} custom-call(bf16[8,64,256]{2,1,0:T(8,128)(2,1)} %cap_any.1, s32[2,128]{1,0:T(2,128)} %grid_any.1, s32[1,64]{1,0:T(1,128)} %bitcast.1, s32[3,512]{1,0:T(4,128)} %vox_any.1), custom_call_target="tpu_custom_call" | custom-call | tf_op jit(solution)/shard_map/pallas_call | solution.py:465
  14.0 0.6 %copy.6 = f32[2,16]{1,0:T(2,128)} copy(f32[2,16]{1,0:T(2,128)S(1)} %shard_map.46) | data formatting | bytes 256

commit v5 on v4

--- a/solution.py
+++ b/solution.py
@@ -262,8 +262,6 @@
         pltpu.make_async_copy(source, target, load_sems.at[i])
         for i, (source, target) in enumerate(pieces)
     ]
-    for load in loads:
-        load.start()
 
     def place(other):
         return lax.div(other, rx_count), lax.rem(other, rx_count)
@@ -287,6 +285,9 @@
         pl.semaphore_signal(
             barrier, inc=1, device_id=place(other), device_id_type=pl.DeviceIdType.MESH
         )
+
+    for load in loads:
+        load.start()
 
     make_table = filter_lanes(exc.shape[1], gate_len)
     pairs = subrun * rx_cols

time: 14.8 us -> 14.8 us (level)
  no operation moved by 1% of the time
where the time goes in v5:
time: 14.8 us; the launch traced here: 14.6 us
  Pallas kernels  14 us (95%)
  local copies, waits for them, and re-layouts  0.56 us (4%)
    pallas_call x1, Pallas kernels, small(): pl.pallas_call(functools.partial(kernel, tx_count, rx_count), out_shape=p...  14 us
    unnamed x1, local copies, waits for them, and re-layouts  0.56 us

profile of v5, /device:TPU:0, one launch (start us, length us, event | category | flops | bytes accessed | tf_op | source)
XLA Modules:
  0.0 14.6 jit_solution(1213846112575587680)
XLA Ops:
  0.0 14.0 %shard_map.46 = f32[2,16]{1,0:T(2,128)S(1)} custom-call(bf16[8,64,256]{2,1,0:T(8,128)(2,1)} %cap_any.1, s32[2,128]{1,0:T(2,128)} %grid_any.1, s32[1,64]{1,0:T(1,128)} %bitcast.1, s32[3,512]{1,0:T(4,128)} %vox_any.1), custom_call_target="tpu_custom_call" | custom-call | tf_op jit(solution)/shard_map/pallas_call | solution.py:466
  14.0 0.6 %copy.6 = f32[2,16]{1,0:T(2,128)} copy(f32[2,16]{1,0:T(2,128)S(1)} %shard_map.46) | data formatting | bytes 256
